TPU v7x, 512 devices: a whole 4x4x16 slice. The times are simulated.
512 devices in a mesh: dp: 8 (over z_hi, core), ctx: 64 (over z_lo, x, y).
Axes of the slice: x: 4, y: 4, z: 16 (z_hi: 4, z_lo: 4; z = z_hi * 4 + z_lo), core: 2. Of those that a mesh axis runs over, the one named last changes fastest.
Arguments:
- inputs: bfloat16 [8, 8192, 4096], P('dp', 'ctx'), may hold values from -0.0234375 to 0.0234375
- grad_out: bfloat16 [8, 8192, 4096], P('dp', 'ctx'), may hold values from -6 to 6
- filt: bfloat16 [8192, 4096], P('ctx'), may hold values from -1.5 to 1.5
Outputs:
- input_grad: bfloat16 [8, 8192, 4096], P('dp', 'ctx')
- filter_grad: float32 [8192, 4096], P('ctx', 'dp')
All inputs are finite; a program needn't handle non-finite values.
Results may differ from a plain program's by a relative error of at most 0.005.
Values may be sent and summed in bfloat16 or wider, within the bound.
A program may use at most 128 MiB of HBM per device.

v0:
```python
import math
import numpy as np
import jax
import jax.numpy as jnp
from jax import lax
from jax.experimental import pallas as pl
from jax.experimental.pallas import tpu as pltpu
from jax.sharding import PartitionSpec as P

N = 16384
KN = 65


def cmul_const(v, c, s):
    re, im = v
    if abs(s) < 1e-12 and abs(c - 1) < 1e-12:
        return v
    if abs(c) < 1e-12 and abs(s - 1) < 1e-12:
        return (-im, re)
    if abs(c) < 1e-12 and abs(s + 1) < 1e-12:
        return (im, -re)
    if abs(abs(c) - abs(s)) < 1e-12:
        h = abs(c)
        sc, ss = (1.0 if c > 0 else -1.0), (1.0 if s > 0 else -1.0)
        a = re * h
        b = im * h
        first = (a if sc > 0 else -a)
        first = first - b if ss > 0 else first + b
        second = (b if sc > 0 else -b)
        second = second + a if ss > 0 else second - a
        return (first, second)
    return (re * c - im * s, re * s + im * c)


def fft_complex(values, sign):
    n = len(values)
    if n == 1:
        return values
    if n == 2:
        (ar, ai), (br, bi) = values
        return [(ar + br, ai + bi), (ar - br, ai - bi)]
    if n % 4 == 0:
        quarter = n // 4
        parts = [fft_complex(values[r::4], sign) for r in range(4)]
        out = [None] * n
        for k in range(quarter):
            turned = []
            for r in range(4):
                angle = sign * 2.0 * math.pi * r * k / n
                turned.append(cmul_const(parts[r][k], math.cos(angle), math.sin(angle)))
            (ar, ai), (br, bi), (cr, ci), (dr, di) = turned
            s0r, s0i, s1r, s1i = ar + cr, ai + ci, ar - cr, ai - ci
            s2r, s2i, s3r, s3i = br + dr, bi + di, br - dr, bi - di
            out[k] = (s0r + s2r, s0i + s2i)
            out[k + 2 * quarter] = (s0r - s2r, s0i - s2i)
            if sign < 0:
                out[k + quarter] = (s1r + s3i, s1i - s3r)
                out[k + 3 * quarter] = (s1r - s3i, s1i + s3r)
            else:
                out[k + quarter] = (s1r - s3i, s1i + s3r)
                out[k + 3 * quarter] = (s1r + s3i, s1i - s3r)
        return out
    half = n // 2
    even = fft_complex(values[0::2], sign)
    odd = fft_complex(values[1::2], sign)
    out = [None] * n
    for k in range(half):
        angle = sign * 2.0 * math.pi * k / n
        tr, ti = cmul_const(odd[k], math.cos(angle), math.sin(angle))
        er, ei = even[k]
        out[k] = (er + tr, ei + ti)
        out[k + half] = (er - tr, ei - ti)
    return out


def odd_bins(values, period):
    quarter = period // 4
    turned = []
    for a in range(quarter):
        angle = -2.0 * math.pi * a / period
        turned.append(cmul_const((values[a], -values[a + quarter]), math.cos(angle), math.sin(angle)))
    spectrum = fft_complex(turned, -1.0)
    found = {}
    for l in range(quarter):
        k = 4 * l + 1
        re, im = spectrum[l]
        if k <= period // 2:
            found[k] = (re, im)
        else:
            found[period - k] = (re, -im)
    return found


def real_bins(values):
    n = len(values)
    if n == 2:
        return {0: (values[0] + values[1], None), 1: (values[0] - values[1], None)}
    half = n // 2
    sums = [values[a] + values[a + half] for a in range(half)]
    diffs = [values[a] - values[a + half] for a in range(half)]
    found = {2 * k: v for k, v in real_bins(sums).items()}
    found.update(odd_bins(diffs, n))
    return found


def padded_bins(values):
    found = odd_bins(values, 2 * len(values))
    found.update({2 * k: v for k, v in real_bins(values).items()})
    return found


def odd_values(bins, period):
    quarter = period // 4
    spectrum = []
    for l in range(quarter):
        k = 4 * l + 1
        if k <= period // 2:
            spectrum.append(bins[k])
        else:
            re, im = bins[period - k]
            spectrum.append((re, -im))
    turned = fft_complex(spectrum, 1.0)
    lower, upper = [], []
    for a in range(quarter):
        angle = 2.0 * math.pi * a / period
        re, im = cmul_const(turned[a], math.cos(angle), math.sin(angle))
        lower.append(re)
        upper.append(-im)
    return lower + upper


def real_values(bins, n):
    if n == 2:
        return [bins[0][0] + bins[1][0], bins[0][0] - bins[1][0]]
    sums = real_values({k // 2: v for k, v in bins.items() if k % 2 == 0}, n // 2)
    diffs = odd_values(bins, n)
    return [s + d for s, d in zip(sums, diffs)] + [s - d for s, d in zip(sums, diffs)]


def padded_values(bins, n):
    odd = odd_values(bins, 2 * n)
    even = real_values({k // 2: v for k, v in bins.items() if k % 2 == 0}, n)
    return [o + e for o, e in zip(odd, even)]


def big_tables():
    m = np.arange(128)
    grid = (m[:, None] * m[None, :] % 128) * (2.0 * np.pi / 128)
    c, s = np.cos(grid), np.sin(grid)
    full = np.block([[c, -s], [s, c]]).astype(np.float32)
    high = full.astype(jnp.bfloat16)
    low = (full - high.astype(np.float32)).astype(jnp.bfloat16)
    turn = np.arange(72)[:, None] * m[None, :] * (2.0 * np.pi / N)
    return high, low, np.cos(turn).astype(np.float32), np.sin(turn).astype(np.float32)


def spectra_of(recv_ref, y_ref, tr_ref, ti_ref, group):
    rows = pl.ds(pl.multiple_of(group * 16, 16), 16)
    values = [recv_ref[a, rows, :].astype(jnp.float32) for a in range(64)]
    bins = padded_bins(values)
    for k in range(KN):
        re, im = bins[k]
        tr, ti = tr_ref[pl.ds(k, 1), :], ti_ref[pl.ds(k, 1), :]
        if im is None:
            re, im = re * tr, -(re * ti)
        else:
            re, im = re * tr + im * ti, im * tr - re * ti
        y_ref[k, rows, pl.ds(0, 128)] = re.astype(jnp.bfloat16)
        y_ref[k, rows, pl.ds(128, 128)] = im.astype(jnp.bfloat16)


def dot_t(x, table):
    return lax.dot_general(x, table, (((1,), (1,)), ((), ())), preferred_element_type=jnp.float32)


def dot_n(x, table):
    return jnp.dot(x, table, preferred_element_type=jnp.float32)


KC = 5


def mix(step, y_ref, hi_ref, lo_ref, v_ref):
    k0 = step * KC
    y = y_ref[pl.ds(k0, KC)].reshape(KC * 160, 256)
    spec = (dot_n(y, hi_ref[...]) + dot_n(y, lo_ref[...])).reshape(KC, 160, 256)
    prods = []
    for i in range(KC):
        k = k0 + i
        ur, ui = spec[i, 0:64, :128], spec[i, 0:64, 128:]
        sr, si = spec[i, 64:128, :128], spec[i, 64:128, 128:]
        kr, ki = spec[i, 128:160, :128], spec[i, 128:160, 128:]
        scale = jnp.where((k == 0) | (k == 64), 1.0 / N, 2.0 / N).astype(jnp.float32)
        ur, ui = ur * scale, ui * scale
        kr = jnp.concatenate([kr, kr], axis=0)
        ki = jnp.concatenate([ki, ki], axis=0)
        pr = kr * ur + ki * ui
        pi = kr * ui - ki * ur
        qr = sr * ur + si * ui
        qi = sr * ui - si * ur
        qr = qr[0:32] + qr[32:64]
        qi = qi[0:32] + qi[32:64]
        re = jnp.concatenate([pr, qr], axis=0)
        im = jnp.concatenate([pi, qi], axis=0)
        prods.append(jnp.concatenate([re, im], axis=1).astype(jnp.bfloat16))
    prod = jnp.concatenate(prods, axis=0)
    back = dot_t(prod, hi_ref[...]) + dot_t(prod, lo_ref[...])
    v_ref[pl.ds(k0, KC)] = back.reshape(KC, 96, 256)


def values_of(v_ref, tr_ref, ti_ref, rows):
    bins = {}
    for k in range(KN):
        re, im = v_ref[k, rows, pl.ds(0, 128)], v_ref[k, rows, pl.ds(128, 128)]
        tr, ti = tr_ref[pl.ds(k, 1), :], ti_ref[pl.ds(k, 1), :]
        if k in (0, 64):
            bins[k] = (re * tr - im * ti, None)
        else:
            bins[k] = (re * tr - im * ti, im * tr + re * ti)
    return padded_values(bins, 64)


def compute_kernel(recv_ref, hi_ref, lo_ref, tr_ref, ti_ref, ig_ref, fg_ref, y_ref, v_ref):
    def first(group, carry):
        spectra_of(recv_ref, y_ref, tr_ref, ti_ref, group)
        return carry

    lax.fori_loop(0, 10, first, 0)

    def second(k, carry):
        mix(k, y_ref, hi_ref, lo_ref, v_ref)
        return carry

    lax.fori_loop(0, KN // KC, second, 0)

    def third(group, carry):
        rows = pl.ds(pl.multiple_of(group * 16, 16), 16)
        out = values_of(v_ref, tr_ref, ti_ref, rows)
        for a in range(64):
            ig_ref[a, group // 2, pl.ds(pl.multiple_of((group % 2) * 16, 16), 16), :] = out[a].astype(jnp.bfloat16)
        return carry

    lax.fori_loop(0, 4, third, 0)

    def fourth(group, carry):
        rows = pl.ds(pl.multiple_of(64 + group * 16, 16), 16)
        out = values_of(v_ref, tr_ref, ti_ref, rows)
        for a in range(0, 64, 2):
            for h in range(2):
                pair = jnp.concatenate([out[a][8 * h:8 * h + 8], out[a + 1][8 * h:8 * h + 8]], axis=0)
                fg_ref[2 * group + h, a // 2, :, :] = pair.astype(jnp.bfloat16)
        return carry

    lax.fori_loop(0, 2, fourth, 0)


def compute_call(recv):
    tables = [jnp.asarray(t) for t in big_tables()]
    return pl.pallas_call(
        compute_kernel,
        out_shape=(
            jax.ShapeDtypeStruct((64, 2, 32, 128), jnp.bfloat16),
            jax.ShapeDtypeStruct((4, 32, 16, 128), jnp.bfloat16),
        ),
        in_specs=[vmem()] * 5,
        out_specs=(vmem(), vmem()),
        scratch_shapes=[
            pltpu.VMEM((KN, 160, 256), jnp.bfloat16),
            pltpu.VMEM((KN, 96, 256), jnp.float32),
        ],
        compiler_params=pltpu.CompilerParams(vmem_limit_bytes=56 * 1024 * 1024),
    )(recv, *tables)


def copy_to(src, dst, send_sem, recv_sem, dp, ctx):
    return pltpu.make_async_remote_copy(
        src_ref=src,
        dst_ref=dst,
        send_sem=send_sem,
        recv_sem=recv_sem,
        device_id=(dp, ctx),
        device_id_type=pl.DeviceIdType.MESH,
    )


def wait_bytes(ref, sem):
    pltpu.make_async_copy(ref, ref, sem).wait()


def partner(me, i):
    return ((me // 16 + i % 4) % 4) * 16 + (me % 16 + i // 4) % 16


def to_pieces(x_ref, st_ref, g, j, index):
    parts = []
    for q in range(4):
        cols = pl.ds(pl.multiple_of(512 * (2 * q + j) + 128 * g, 128), 128)
        parts.append(x_ref[:, cols].astype(jnp.float32).T.reshape(16, 8, 128))
    owners = pl.ds(pl.multiple_of(16 * g, 16), 16)
    index(owners)[...] = jnp.concatenate(parts, axis=1).astype(jnp.bfloat16)


def gather_kernel(up_ref, sig_ref, filt_ref, out_ref, up_st, sig_st, filt_st, send_sem, recv_sem):
    dp = lax.axis_index("dp")
    me = lax.axis_index("ctx")
    core, high = dp % 2, dp // 2

    def send_signal(which, x_ref, st_ref):
        def turn(i, carry):
            g, j = i // 2, i % 2
            to_pieces(x_ref, st_ref, g, j, lambda owners: st_ref.at[owners, j])
            return carry

        lax.fori_loop(0, 8, turn, 0)
        rows = pl.ds(pl.multiple_of(64 * which + 32 * core, 32), 32)
        pltpu.make_async_copy(st_ref.at[me, core], out_ref.at[me, rows], recv_sem.at[which]).start()
        copy_to(
            st_ref.at[me, 1 - core], out_ref.at[me, rows], send_sem.at[which], recv_sem.at[which],
            2 * high + 1 - core, me,
        ).start()

        def send(i, carry):
            c = partner(me, i)
            for j in range(2):
                copy_to(
                    st_ref.at[c, j], out_ref.at[me, rows], send_sem.at[which], recv_sem.at[which],
                    2 * high + j, c,
                ).start()
            return carry

        lax.fori_loop(1, 64, send, 0)

    def send_filter():
        def turn(g, carry):
            to_pieces(filt_ref, filt_st, g, core, lambda owners: filt_st.at[owners])
            return carry

        lax.fori_loop(0, 4, turn, 0)
        rows = pl.ds(128, 32)
        pltpu.make_async_copy(filt_st.at[me], out_ref.at[me, rows], recv_sem.at[2]).start()

        def send(i, carry):
            c = partner(me, i)
            copy_to(
                filt_st.at[c], out_ref.at[me, rows], send_sem.at[2], recv_sem.at[2], dp, c
            ).start()
            return carry

        lax.fori_loop(1, 64, send, 0)

    send_signal(0, up_ref, up_st)
    send_filter()
    send_signal(1, sig_ref, sig_st)
    for which, rows in ((0, pl.ds(0, 64)), (1, pl.ds(64, 64)), (2, pl.ds(128, 32))):
        wait_bytes(out_ref.at[:, rows], recv_sem.at[which])
    for which, st_ref in ((0, up_st), (1, sig_st)):
        wait_bytes(st_ref.at[pl.ds(0, 63)], send_sem.at[which])
        wait_bytes(st_ref.at[0, 0], send_sem.at[which])
    wait_bytes(filt_st.at[pl.ds(0, 63)], send_sem.at[2])


def scatter_kernel(
    ig_ref, fg_ref, ig_out, fg_out, ig_in, fg_in, total, fg_parts, send_sem, recv_sem
):
    dp = lax.axis_index("dp")
    me = lax.axis_index("ctx")
    core, high = dp % 2, dp // 2
    for step in range(1, 4):
        q = (high + step) % 4
        copy_to(
            fg_ref.at[q], fg_in.at[high], send_sem.at[0], recv_sem.at[0], 2 * q + core, me
        ).start()
    pltpu.make_async_copy(ig_ref.at[me, core], ig_in.at[me, core], recv_sem.at[1]).start()
    copy_to(
        ig_ref.at[me, 1 - core], ig_in.at[me, core], send_sem.at[1], recv_sem.at[1],
        2 * high + 1 - core, me,
    ).start()

    def send(i, carry):
        c = partner(me, i)
        for j in range(2):
            copy_to(
                ig_ref.at[c, j], ig_in.at[me, core], send_sem.at[1], recv_sem.at[1],
                2 * high + j, c,
            ).start()
        return carry

    lax.fori_loop(1, 64, send, 0)
    wait_bytes(fg_in.at[pl.ds(0, 3)], recv_sem.at[0])

    def add(p, carry):
        terms = fg_ref[high, p].astype(jnp.float32)
        for step in range(1, 4):
            terms = terms + fg_in[(high + step) % 4, p].astype(jnp.float32)
        total[2 * p] = terms[0:8]
        total[2 * p + 1] = terms[8:16]
        return carry

    lax.fori_loop(0, 32, add, 0)
    pltpu.make_async_copy(total.at[me], fg_parts.at[me], recv_sem.at[2]).start()

    def send_total(i, carry):
        c = partner(me, i)
        copy_to(total.at[c], fg_parts.at[me], send_sem.at[2], recv_sem.at[2], dp, c).start()
        return carry

    lax.fori_loop(1, 64, send_total, 0)
    wait_bytes(ig_in, recv_sem.at[1])

    def turn(i, carry):
        g, j = i // 2, i % 2
        owners = pl.ds(pl.multiple_of(16 * g, 16), 16)
        block = ig_in[owners, j].astype(jnp.float32)
        for q in range(4):
            cols = pl.ds(pl.multiple_of(512 * (2 * q + j) + 128 * g, 128), 128)
            part = block[:, 8 * q : 8 * q + 8, :].reshape(128, 128)
            ig_out[:, cols] = part.T.astype(jnp.bfloat16)
        return carry

    lax.fori_loop(0, 8, turn, 0)
    wait_bytes(fg_parts, recv_sem.at[2])
    for g in range(4):
        part = fg_parts[pl.ds(16 * g, 16)].reshape(128, 128)
        fg_out[:, pl.ds(128 * g, 128)] = part.T
    wait_bytes(fg_in.at[pl.ds(0, 3)], send_sem.at[0])
    wait_bytes(ig_in.at[pl.ds(0, 63)], send_sem.at[1])
    wait_bytes(ig_in.at[0, 0], send_sem.at[1])
    wait_bytes(fg_parts.at[pl.ds(0, 63)], send_sem.at[2])


def vmem():
    return pl.BlockSpec(memory_space=pltpu.VMEM)


def gather_call(up, sig, filt):
    return pl.pallas_call(
        gather_kernel,
        out_shape=jax.ShapeDtypeStruct((64, 160, 128), jnp.bfloat16),
        in_specs=[vmem()] * 3,
        out_specs=pl.BlockSpec(memory_space=pl.ANY),
        scratch_shapes=[
            pltpu.VMEM((64, 2, 32, 128), jnp.bfloat16),
            pltpu.VMEM((64, 2, 32, 128), jnp.bfloat16),
            pltpu.VMEM((64, 32, 128), jnp.bfloat16),
            pltpu.SemaphoreType.DMA((3,)),
            pltpu.SemaphoreType.DMA((3,)),
        ],
        compiler_params=pltpu.CompilerParams(
            has_side_effects=True, vmem_limit_bytes=32 * 1024 * 1024
        ),
    )(up, sig, filt)


def scatter_call(ig, fg):
    return pl.pallas_call(
        scatter_kernel,
        out_shape=(
            jax.ShapeDtypeStruct((128, 4096), jnp.bfloat16),
            jax.ShapeDtypeStruct((128, 512), jnp.float32),
        ),
        in_specs=[vmem()] * 2,
        out_specs=(vmem(), vmem()),
        scratch_shapes=[
            pltpu.VMEM((64, 2, 32, 128), jnp.bfloat16),
            pltpu.VMEM((4, 32, 16, 128), jnp.bfloat16),
            pltpu.VMEM((64, 8, 128), jnp.float32),
            pltpu.VMEM((64, 8, 128), jnp.float32),
            pltpu.SemaphoreType.DMA((3,)),
            pltpu.SemaphoreType.DMA((3,)),
        ],
        compiler_params=pltpu.CompilerParams(
            has_side_effects=True, vmem_limit_bytes=32 * 1024 * 1024
        ),
    )(ig, fg)


def shards(inputs, grad_out, filt):
    recv = gather_call(grad_out[0], inputs[0], filt)
    ig, fg = compute_call(recv)
    input_grad, filter_grad = scatter_call(ig, fg)
    return input_grad[None], filter_grad


def solution(mesh):
    in_specs = (P("dp", "ctx", None), P("dp", "ctx", None), P("ctx", None))
    out_specs = (P("dp", "ctx", None), P("ctx", "dp"))
    return jax.shard_map(shards, mesh=mesh, in_specs=in_specs, out_specs=out_specs, check_vma=False)
```

profile of v0, /device:TPU:1, one launch (start us, length us, event | category | flops | bytes accessed | tf_op | source)
XLA Modules:
  0.0 188.2 jit_solution(4305104018185396743)
XLA Ops:
  0.6 0.0 copy-start.2
  0.6 1.2 copy-done.2
  1.9 0.0 copy-start.3
  1.9 1.2 copy-done.3
  3.1 0.0 copy-start.4
  3.1 1.2 copy-done.4
  4.3 84.0 %shard_map.86.recv_ref = bf16[64,160,128]{2,1,0:T(8,128)(2,1)S(1)} custom-call(bf16[128,4096]{1,0:T(8,128)(2,1)S(1)} %bitcast.4, bf16[128,4096]{1,0:T(8,128)(2,1)S(1)} %bitcast.5, bf16[128,4096]{1,0:T(8,128)(2,1)S(1)} %copy-done.4), custom_call_target="tpu_custom_call" | custom-call | tf_op jit(solution)/shard_map/pallas_call | solution.py:436
  88.3 0.0 copy-start
  88.3 1.5 copy-done
  89.8 21.9 %shard_map.87 = (bf16[64,2,32,128]{3,2,1,0:T(8,128)(2,1)}, bf16[4,32,16,128]{3,2,1,0:T(8,128)(2,1)}) custom-call(bf16[64,160,128]{2,1,0:T(8,128)(2,1)} %copy-done, bf16[256,256]{1,0:T(8,128)(2,1)} %constant.8.clone.hi_ref, bf16[256,256]{1,0:T(8,128)(2,1)} %constant.9.clone.lo_ref, f32[72,128]{1,0:T(8,128)} %constant.10.clone.tr_ref, ...), custom_call_target="tpu_custom_call" | custom-call | tf_op jit(solution)/shard_map/pallas_call | solution.py:259
  111.7 0.0 copy-start.1
  111.7 1.2 copy-done.1
  113.0 0.0 copy-start.5
  113.0 1.0 copy-done.5
  114.0 72.5 %shard_map.88 = (bf16[128,4096]{1,0:T(8,128)(2,1)S(1)}, f32[128,512]{1,0:T(8,128)S(1)}) custom-call(bf16[64,2,32,128]{3,2,1,0:T(8,128)(2,1)S(1)} %copy-done.1, bf16[4,32,16,128]{3,2,1,0:T(8,128)(2,1)S(1)} %copy-done.5), custom_call_target="tpu_custom_call" | custom-call | tf_op jit(solution)/shard_map/pallas_call | solution.py:455
  186.5 1.0 copy.11
  187.5 0.7 copy.12
Async XLA Ops:
  0.6 1.2 copy-start.2
  1.9 1.2 copy-start.3
  3.1 1.2 copy-start.4
  88.3 1.5 copy-start
  111.7 1.2 copy-start.1
  113.0 1.0 copy-start.5
where the time goes:
time: 189 us; the launch traced here: 188 us
  Pallas kernels  178 us (94%)
  local copies, waits for them, and re-layouts  9.12 us (5%)
    pallas_call x1, Pallas kernels, gather_call(): pl.pallas_call(gather_kernel, out_shape=jax.ShapeDtypeStruct((64, 160, 12...  84 us
    pallas_call x1, Pallas kernels, scatter_call(): pl.pallas_call(scatter_kernel, out_shape=(jax.ShapeDtypeStruct((128, 4096...  72.5 us
    pallas_call x1, Pallas kernels, compute_call(): pl.pallas_call(compute_kernel, out_shape=(jax.ShapeDtypeStruct((64, 2, 32...  21.9 us
    unnamed x14, local copies, waits for them, and re-layouts  9.12 us

commit v1 on v0

v1 whole, which is shorter than its diff:
```python
import math
import numpy as np
import jax
import jax.numpy as jnp
from jax import lax
from jax.experimental import pallas as pl
from jax.experimental.pallas import tpu as pltpu
from jax.sharding import PartitionSpec as P

N = 16384
KN = 65
KC = 5


def cmul_const(v, c, s):
    re, im = v
    if abs(s) < 1e-12 and abs(c - 1) < 1e-12:
        return v
    if abs(c) < 1e-12 and abs(s - 1) < 1e-12:
        return (-im, re)
    if abs(c) < 1e-12 and abs(s + 1) < 1e-12:
        return (im, -re)
    if abs(abs(c) - abs(s)) < 1e-12:
        h = abs(c)
        sc, ss = (1.0 if c > 0 else -1.0), (1.0 if s > 0 else -1.0)
        a = re * h
        b = im * h
        first = (a if sc > 0 else -a)
        first = first - b if ss > 0 else first + b
        second = (b if sc > 0 else -b)
        second = second + a if ss > 0 else second - a
        return (first, second)
    return (re * c - im * s, re * s + im * c)


def fft_complex(values, sign):
    n = len(values)
    if n == 1:
        return values
    if n == 2:
        (ar, ai), (br, bi) = values
        return [(ar + br, ai + bi), (ar - br, ai - bi)]
    if n % 4 == 0:
        quarter = n // 4
        parts = [fft_complex(values[r::4], sign) for r in range(4)]
        out = [None] * n
        for k in range(quarter):
            turned = []
            for r in range(4):
                angle = sign * 2.0 * math.pi * r * k / n
                turned.append(cmul_const(parts[r][k], math.cos(angle), math.sin(angle)))
            (ar, ai), (br, bi), (cr, ci), (dr, di) = turned
            s0r, s0i, s1r, s1i = ar + cr, ai + ci, ar - cr, ai - ci
            s2r, s2i, s3r, s3i = br + dr, bi + di, br - dr, bi - di
            out[k] = (s0r + s2r, s0i + s2i)
            out[k + 2 * quarter] = (s0r - s2r, s0i - s2i)
            if sign < 0:
                out[k + quarter] = (s1r + s3i, s1i - s3r)
                out[k + 3 * quarter] = (s1r - s3i, s1i + s3r)
            else:
                out[k + quarter] = (s1r - s3i, s1i + s3r)
                out[k + 3 * quarter] = (s1r + s3i, s1i - s3r)
        return out
    half = n // 2
    even = fft_complex(values[0::2], sign)
    odd = fft_complex(values[1::2], sign)
    out = [None] * n
    for k in range(half):
        angle = sign * 2.0 * math.pi * k / n
        tr, ti = cmul_const(odd[k], math.cos(angle), math.sin(angle))
        er, ei = even[k]
        out[k] = (er + tr, ei + ti)
        out[k + half] = (er - tr, ei - ti)
    return out


def odd_bins(values, period):
    quarter = period // 4
    turned = []
    for a in range(quarter):
        angle = -2.0 * math.pi * a / period
        turned.append(cmul_const((values[a], -values[a + quarter]), math.cos(angle), math.sin(angle)))
    spectrum = fft_complex(turned, -1.0)
    found = {}
    for l in range(quarter):
        k = 4 * l + 1
        re, im = spectrum[l]
        if k <= period // 2:
            found[k] = (re, im)
        else:
            found[period - k] = (re, -im)
    return found


def real_bins(values):
    n = len(values)
    if n == 2:
        return {0: (values[0] + values[1], None), 1: (values[0] - values[1], None)}
    half = n // 2
    sums = [values[a] + values[a + half] for a in range(half)]
    diffs = [values[a] - values[a + half] for a in range(half)]
    found = {2 * k: v for k, v in real_bins(sums).items()}
    found.update(odd_bins(diffs, n))
    return found


def padded_bins(values):
    found = odd_bins(values, 2 * len(values))
    found.update({2 * k: v for k, v in real_bins(values).items()})
    return found


def odd_values(bins, period):
    quarter = period // 4
    spectrum = []
    for l in range(quarter):
        k = 4 * l + 1
        if k <= period // 2:
            spectrum.append(bins[k])
        else:
            re, im = bins[period - k]
            spectrum.append((re, -im))
    turned = fft_complex(spectrum, 1.0)
    lower, upper = [], []
    for a in range(quarter):
        angle = 2.0 * math.pi * a / period
        re, im = cmul_const(turned[a], math.cos(angle), math.sin(angle))
        lower.append(re)
        upper.append(-im)
    return lower + upper


def real_values(bins, n):
    if n == 2:
        return [bins[0][0] + bins[1][0], bins[0][0] - bins[1][0]]
    sums = real_values({k // 2: v for k, v in bins.items() if k % 2 == 0}, n // 2)
    diffs = odd_values(bins, n)
    return [s + d for s, d in zip(sums, diffs)] + [s - d for s, d in zip(sums, diffs)]


def padded_values(bins, n):
    odd = odd_values(bins, 2 * n)
    even = real_values({k // 2: v for k, v in bins.items() if k % 2 == 0}, n)
    return [o + e for o, e in zip(odd, even)]


def big_tables():
    m = np.arange(128)
    grid = (m[:, None] * m[None, :] % 128) * (2.0 * np.pi / 128)
    c, s = np.cos(grid), np.sin(grid)
    full = np.block([[c, -s], [s, c]]).astype(np.float32)
    high = full.astype(jnp.bfloat16)
    low = (full - high.astype(np.float32)).astype(jnp.bfloat16)
    turn = np.arange(72)[:, None] * m[None, :] * (2.0 * np.pi / N)
    return high, low, np.cos(turn).astype(np.float32), np.sin(turn).astype(np.float32)


def spectra_of(src_ref, y_ref, first, tr_ref, ti_ref, group):
    rows = pl.ds(pl.multiple_of(group * 16, 16), 16)
    kept = pl.ds(pl.multiple_of(first + group * 16, 16), 16)
    bins = padded_bins([src_ref[a, rows, :].astype(jnp.float32) for a in range(64)])
    for k in range(KN):
        re, im = bins[k]
        tr, ti = tr_ref[pl.ds(k, 1), :], ti_ref[pl.ds(k, 1), :]
        if im is None:
            re, im = re * tr, -(re * ti)
        else:
            re, im = re * tr + im * ti, im * tr - re * ti
        y_ref[k, kept, pl.ds(0, 128)] = re.astype(jnp.bfloat16)
        y_ref[k, kept, pl.ds(128, 128)] = im.astype(jnp.bfloat16)


def forward_dot(y_ref, k0, first, rows, hi_ref, lo_ref):
    y = y_ref[pl.ds(k0, KC), pl.ds(first, rows), :].reshape(KC * rows, 256)
    spec = jnp.dot(y, hi_ref[...], preferred_element_type=jnp.float32)
    spec = spec + jnp.dot(y, lo_ref[...], preferred_element_type=jnp.float32)
    return spec.reshape(KC, rows, 256)


def inverse_dot(prods, hi_ref, lo_ref):
    prod = jnp.concatenate(prods, axis=0)
    form = (((1,), (1,)), ((), ()))
    back = lax.dot_general(prod, hi_ref[...], form, preferred_element_type=jnp.float32)
    back = back + lax.dot_general(prod, lo_ref[...], form, preferred_element_type=jnp.float32)
    return back.reshape(KC, prod.shape[0] // KC, 256)


def conj_product(x, u):
    xr, xi = x[:, :128], x[:, 128:]
    ur, ui = u[:, :128], u[:, 128:]
    return xr * ur + xi * ui, xr * ui - xi * ur


def values_of(v_ref, tr_ref, ti_ref, rows):
    bins = {}
    for k in range(KN):
        re, im = v_ref[k, rows, pl.ds(0, 128)], v_ref[k, rows, pl.ds(128, 128)]
        tr, ti = tr_ref[pl.ds(k, 1), :], ti_ref[pl.ds(k, 1), :]
        if k in (0, 64):
            bins[k] = (re * tr - im * ti, None)
        else:
            bins[k] = (re * tr - im * ti, im * tr + re * ti)
    return padded_values(bins, 64)


def copy_to(src, dst, send_sem, recv_sem, dp, ctx):
    return pltpu.make_async_remote_copy(
        src_ref=src,
        dst_ref=dst,
        send_sem=send_sem,
        recv_sem=recv_sem,
        device_id=(dp, ctx),
        device_id_type=pl.DeviceIdType.MESH,
    )


def wait_bytes(ref, sem):
    pltpu.make_async_copy(ref, ref, sem).wait()


def partner(me, i):
    return ((me // 16 + i % 4) % 4) * 16 + (me % 16 + i // 4) % 16


def to_pieces(x_ref, st_ref, g, j, index):
    parts = []
    for q in range(4):
        cols = pl.ds(pl.multiple_of(512 * (2 * q + j) + 128 * g, 128), 128)
        parts.append(x_ref[:, cols].astype(jnp.float32).T.reshape(16, 8, 128))
    owners = pl.ds(pl.multiple_of(16 * g, 16), 16)
    index(owners)[...] = jnp.concatenate(parts, axis=1).astype(jnp.bfloat16)


def loop(start, stop, step):
    def run(i, carry):
        step(i)
        return carry

    lax.fori_loop(start, stop, run, 0)


def fused_kernel(
    up_hbm, sig_hbm, filt_hbm, hi_ref, lo_ref, tr_ref, ti_ref,
    ig_out, fg_out,
    up_x, sig_x, filt_x, up_st, sig_st, filt_st, up_in, sig_in, filt_in,
    y_ref, u_ref, v_ref, ig_st, fg_st, ig_in, fg_in, total, fg_parts,
    load_sem, send_sem, recv_sem,
):
    dp = lax.axis_index("dp")
    me = lax.axis_index("ctx")
    core, high = dp % 2, dp // 2
    mesh_id = pl.DeviceIdType.MESH
    loads = [
        pltpu.make_async_copy(src, dst, load_sem.at[i])
        for i, (src, dst) in enumerate(((up_hbm, up_x), (sig_hbm, sig_x), (filt_hbm, filt_x)))
    ]
    for load in loads:
        load.start()
    barrier = pltpu.get_barrier_semaphore()
    pl.semaphore_signal(barrier, inc=1, device_id=(2 * high + 1 - core, me), device_id_type=mesh_id)
    for step in range(1, 4):
        pl.semaphore_signal(
            barrier, inc=1, device_id=(2 * ((high + step) % 4) + core, me), device_id_type=mesh_id
        )

    def greet(i):
        c = partner(me, i)
        for j in range(2):
            pl.semaphore_signal(barrier, inc=1, device_id=(2 * high + j, c), device_id_type=mesh_id)

    loop(1, 64, greet)

    def turn_signal(x_ref, st_ref):
        def turn(i):
            g, j = i // 2, i % 2
            to_pieces(x_ref, st_ref, g, j, lambda owners: st_ref.at[owners, j])

        loop(0, 8, turn)

    def spread(src_ref, dst_ref, slot, which):
        pltpu.make_async_copy(src_ref.at[me, core], dst_ref.at[slot], recv_sem.at[which]).start()
        copy_to(
            src_ref.at[me, 1 - core], dst_ref.at[slot], send_sem.at[which], recv_sem.at[which],
            2 * high + 1 - core, me,
        ).start()

        def send(i):
            c = partner(me, i)
            for j in range(2):
                copy_to(
                    src_ref.at[c, j], dst_ref.at[slot], send_sem.at[which], recv_sem.at[which],
                    2 * high + j, c,
                ).start()

        loop(1, 64, send)

    def spread_same(src_ref, dst_ref, which):
        pltpu.make_async_copy(src_ref.at[me], dst_ref.at[me], recv_sem.at[which]).start()

        def send(i):
            c = partner(me, i)
            copy_to(
                src_ref.at[c], dst_ref.at[me], send_sem.at[which], recv_sem.at[which], dp, c
            ).start()

        loop(1, 64, send)

    loads[0].wait()
    turn_signal(up_x, up_st)
    pl.semaphore_wait(barrier, 130)
    mine = (me, pl.ds(pl.multiple_of(32 * core, 32), 32))
    spread(up_st, up_in, mine, 0)
    loads[1].wait()
    turn_signal(sig_x, sig_st)
    spread(sig_st, sig_in, mine, 1)
    loads[2].wait()
    loop(0, 4, lambda g: to_pieces(filt_x, filt_st, g, core, lambda owners: filt_st.at[owners]))
    spread_same(filt_st, filt_in, 2)

    wait_bytes(up_in, recv_sem.at[0])
    loop(0, 4, lambda g: spectra_of(up_in, y_ref, 0, tr_ref, ti_ref, g))

    def up_spectra(step):
        k0 = step * KC
        spec = forward_dot(y_ref, k0, 0, 64, hi_ref, lo_ref)
        for i in range(KC):
            k = k0 + i
            scale = jnp.where((k == 0) | (k == 64), 1.0 / N, 2.0 / N).astype(jnp.float32)
            u_ref[k] = spec[i] * scale

    loop(0, KN // KC, up_spectra)

    wait_bytes(sig_in, recv_sem.at[1])
    loop(0, 4, lambda g: spectra_of(sig_in, y_ref, 64, tr_ref, ti_ref, g))

    def filter_products(step):
        k0 = step * KC
        spec = forward_dot(y_ref, k0, 64, 64, hi_ref, lo_ref)
        prods = []
        for i in range(KC):
            re, im = conj_product(spec[i], u_ref[k0 + i])
            re, im = re[0:32] + re[32:64], im[0:32] + im[32:64]
            prods.append(jnp.concatenate([re, im], axis=1).astype(jnp.bfloat16))
        v_ref[pl.ds(k0, KC), pl.ds(64, 32), :] = inverse_dot(prods, hi_ref, lo_ref)

    loop(0, KN // KC, filter_products)

    def filter_values(group):
        rows = pl.ds(pl.multiple_of(64 + group * 16, 16), 16)
        out = values_of(v_ref, tr_ref, ti_ref, rows)
        for a in range(0, 64, 2):
            for h in range(2):
                pair = jnp.concatenate([out[a][8 * h:8 * h + 8], out[a + 1][8 * h:8 * h + 8]], axis=0)
                fg_st[2 * group + h, a // 2, :, :] = pair.astype(jnp.bfloat16)

    loop(0, 2, filter_values)
    for step in range(1, 4):
        q = (high + step) % 4
        copy_to(fg_st.at[q], fg_in.at[high], send_sem.at[3], recv_sem.at[3], 2 * q + core, me).start()

    wait_bytes(filt_in, recv_sem.at[2])
    loop(0, 2, lambda g: spectra_of(filt_in, y_ref, 128, tr_ref, ti_ref, g))

    def input_products(step):
        k0 = step * KC
        spec = forward_dot(y_ref, k0, 128, 32, hi_ref, lo_ref)
        prods = []
        for i in range(KC):
            both = jnp.concatenate([spec[i], spec[i]], axis=0)
            re, im = conj_product(both, u_ref[k0 + i])
            prods.append(jnp.concatenate([re, im], axis=1).astype(jnp.bfloat16))
        v_ref[pl.ds(k0, KC), pl.ds(0, 64), :] = inverse_dot(prods, hi_ref, lo_ref)

    loop(0, KN // KC, input_products)

    def input_values(group):
        rows = pl.ds(pl.multiple_of(group * 16, 16), 16)
        out = values_of(v_ref, tr_ref, ti_ref, rows)
        kept = pl.ds(pl.multiple_of((group % 2) * 16, 16), 16)
        for a in range(64):
            ig_st[a, group // 2, kept, :] = out[a].astype(jnp.bfloat16)

    loop(0, 4, input_values)
    spread(ig_st, ig_in, (me, core), 4)

    wait_bytes(fg_in.at[pl.ds(0, 3)], recv_sem.at[3])

    def add(p):
        terms = fg_st[high, p].astype(jnp.float32)
        for step in range(1, 4):
            terms = terms + fg_in[(high + step) % 4, p].astype(jnp.float32)
        total[2 * p] = terms[0:8]
        total[2 * p + 1] = terms[8:16]

    loop(0, 32, add)
    spread_same(total, fg_parts, 5)
    wait_bytes(ig_in, recv_sem.at[4])

    def turn_back(i):
        g, j = i // 2, i % 2
        owners = pl.ds(pl.multiple_of(16 * g, 16), 16)
        block = ig_in[owners, j].astype(jnp.float32)
        for q in range(4):
            cols = pl.ds(pl.multiple_of(512 * (2 * q + j) + 128 * g, 128), 128)
            part = block[:, 8 * q : 8 * q + 8, :].reshape(128, 128)
            ig_out[:, cols] = part.T.astype(jnp.bfloat16)

    loop(0, 8, turn_back)
    wait_bytes(fg_parts, recv_sem.at[5])
    for g in range(4):
        part = fg_parts[pl.ds(16 * g, 16)].reshape(128, 128)
        fg_out[:, pl.ds(128 * g, 128)] = part.T
    for which in (0, 1, 4):
        wait_bytes(ig_in.at[pl.ds(0, 63)], send_sem.at[which])
        wait_bytes(ig_in.at[0, 0], send_sem.at[which])
    wait_bytes(filt_in.at[pl.ds(0, 63)], send_sem.at[2])
    wait_bytes(fg_in.at[pl.ds(0, 3)], send_sem.at[3])
    wait_bytes(fg_parts.at[pl.ds(0, 63)], send_sem.at[5])


def shards(inputs, grad_out, filt):
    vmem = pl.BlockSpec(memory_space=pltpu.VMEM)
    hbm = pl.BlockSpec(memory_space=pl.ANY)
    tables = [jnp.asarray(t) for t in big_tables()]
    bf16, f32 = jnp.bfloat16, jnp.float32
    input_grad, filter_grad = pl.pallas_call(
        fused_kernel,
        out_shape=(
            jax.ShapeDtypeStruct((128, 4096), bf16),
            jax.ShapeDtypeStruct((128, 512), f32),
        ),
        in_specs=[hbm] * 3 + [vmem] * 4,
        out_specs=(vmem, vmem),
        scratch_shapes=[
            pltpu.VMEM((128, 4096), bf16),
            pltpu.VMEM((128, 4096), bf16),
            pltpu.VMEM((128, 4096), bf16),
            pltpu.VMEM((64, 2, 32, 128), bf16),
            pltpu.VMEM((64, 2, 32, 128), bf16),
            pltpu.VMEM((64, 32, 128), bf16),
            pltpu.VMEM((64, 64, 128), bf16),
            pltpu.VMEM((64, 64, 128), bf16),
            pltpu.VMEM((64, 32, 128), bf16),
            pltpu.VMEM((KN, 160, 256), bf16),
            pltpu.VMEM((KN, 64, 256), f32),
            pltpu.VMEM((KN, 96, 256), f32),
            pltpu.VMEM((64, 2, 32, 128), bf16),
            pltpu.VMEM((4, 32, 16, 128), bf16),
            pltpu.VMEM((64, 2, 32, 128), bf16),
            pltpu.VMEM((4, 32, 16, 128), bf16),
            pltpu.VMEM((64, 8, 128), f32),
            pltpu.VMEM((64, 8, 128), f32),
            pltpu.SemaphoreType.DMA((3,)),
            pltpu.SemaphoreType.DMA((6,)),
            pltpu.SemaphoreType.DMA((6,)),
        ],
        compiler_params=pltpu.CompilerParams(
            collective_id=0, has_side_effects=True, vmem_limit_bytes=50 * 1024 * 1024
        ),
    )(grad_out[0], inputs[0], filt, *tables)
    return input_grad[None], filter_grad


def solution(mesh):
    in_specs = (P("dp", "ctx", None), P("dp", "ctx", None), P("ctx", None))
    out_specs = (P("dp", "ctx", None), P("ctx", "dp"))
    return jax.shard_map(shards, mesh=mesh, in_specs=in_specs, out_specs=out_specs, check_vma=False)
```

time: 189 us -> 145 us (0.77)
  Pallas kernels: 178 us -> 137 us
    pallas_call x3 -> x1, Pallas kernels: 178 us -> 137 us  [shards(): pl.pallas_call(fused_kernel, out_shape=(jax.ShapeDtypeStruct((128, 4096),...]
where the time goes in v1:
time: 145 us
  Pallas kernels  137 us (94%)
  local copies, waits for them, and re-layouts  7.46 us (5%)
    pallas_call x1, Pallas kernels, shards(): pl.pallas_call(fused_kernel, out_shape=(jax.ShapeDtypeStruct((128, 4096),...  137 us
    unnamed x14, local copies, waits for them, and re-layouts  7.46 us

profile of v1, /device:TPU:1, one launch (start us, length us, event | category | flops | bytes accessed | tf_op | source)
XLA Modules:
  0.0 144.7 jit_solution(5647031889855244491)
XLA Ops:
  0.6 0.0 copy-start
  0.6 1.2 copy-done
  1.9 0.0 copy-start.1
  1.9 1.2 copy-done.1
  3.1 0.0 copy-start.2
  3.1 0.9 copy-done.2
  4.0 0.0 copy-start.3
  4.0 0.9 copy-done.3
  4.9 0.0 copy-start.4
  4.9 0.8 copy-done.4
  5.7 0.0 copy-start.5
  5.7 0.8 copy-done.5
  6.4 136.5 %shard_map.86 = (bf16[128,4096]{1,0:T(8,128)(2,1)S(1)}, f32[128,512]{1,0:T(8,128)S(1)}) custom-call(bf16[128,4096]{1,0:T(8,128)(2,1)S(1)} %bitcast.3, bf16[128,4096]{1,0:T(8,128)(2,1)S(1)} %bitcast.4, bf16[128,4096]{1,0:T(8,128)(2,1)} %filt_hbm.1, bf16[256,256]{1,0:T(8,128)(2,1)S(1)} %copy-done.3, bf16[256,256]{1,0:T(8,128)(2,1)S(1)} %copy-done.2, ...), custom_call_target="tpu_custom_call" | custom-call | tf_op jit(solution)/shard_map/pallas_call | solution.py:426
  143.0 1.0 copy.11
  144.0 0.7 copy.12
Async XLA Ops:
  0.6 1.2 copy-start
  1.9 1.2 copy-start.1
  3.1 0.9 copy-start.2
  4.0 0.9 copy-start.3
  4.9 0.8 copy-start.4
  5.7 0.8 copy-start.5

commit v2 on v1

--- a/solution.py
+++ b/solution.py
@@ -152,16 +152,16 @@
     high = full.astype(jnp.bfloat16)
     low = (full - high.astype(np.float32)).astype(jnp.bfloat16)
     turn = np.arange(72)[:, None] * m[None, :] * (2.0 * np.pi / N)
-    return high, low, np.cos(turn).astype(np.float32), np.sin(turn).astype(np.float32)
-
-
-def spectra_of(src_ref, y_ref, first, tr_ref, ti_ref, group):
+    return np.stack([high, low]), np.stack([np.cos(turn), np.sin(turn)]).astype(np.float32)
+
+
+def spectra_of(src_ref, y_ref, first, tw_ref, group):
     rows = pl.ds(pl.multiple_of(group * 16, 16), 16)
     kept = pl.ds(pl.multiple_of(first + group * 16, 16), 16)
     bins = padded_bins([src_ref[a, rows, :].astype(jnp.float32) for a in range(64)])
     for k in range(KN):
         re, im = bins[k]
-        tr, ti = tr_ref[pl.ds(k, 1), :], ti_ref[pl.ds(k, 1), :]
+        tr, ti = tw_ref[0, pl.ds(k, 1), :], tw_ref[1, pl.ds(k, 1), :]
         if im is None:
             re, im = re * tr, -(re * ti)
         else:
@@ -170,18 +170,18 @@
         y_ref[k, kept, pl.ds(128, 128)] = im.astype(jnp.bfloat16)
 
 
-def forward_dot(y_ref, k0, first, rows, hi_ref, lo_ref):
+def forward_dot(y_ref, k0, first, rows, tab_ref):
     y = y_ref[pl.ds(k0, KC), pl.ds(first, rows), :].reshape(KC * rows, 256)
-    spec = jnp.dot(y, hi_ref[...], preferred_element_type=jnp.float32)
-    spec = spec + jnp.dot(y, lo_ref[...], preferred_element_type=jnp.float32)
+    spec = jnp.dot(y, tab_ref[0], preferred_element_type=jnp.float32)
+    spec = spec + jnp.dot(y, tab_ref[1], preferred_element_type=jnp.float32)
     return spec.reshape(KC, rows, 256)
 
 
-def inverse_dot(prods, hi_ref, lo_ref):
+def inverse_dot(prods, tab_ref):
     prod = jnp.concatenate(prods, axis=0)
     form = (((1,), (1,)), ((), ()))
-    back = lax.dot_general(prod, hi_ref[...], form, preferred_element_type=jnp.float32)
-    back = back + lax.dot_general(prod, lo_ref[...], form, preferred_element_type=jnp.float32)
+    back = lax.dot_general(prod, tab_ref[0], form, preferred_element_type=jnp.float32)
+    back = back + lax.dot_general(prod, tab_ref[1], form, preferred_element_type=jnp.float32)
     return back.reshape(KC, prod.shape[0] // KC, 256)
 
 
@@ -191,11 +191,11 @@
     return xr * ur + xi * ui, xr * ui - xi * ur
 
 
-def values_of(v_ref, tr_ref, ti_ref, rows):
+def values_of(v_ref, tw_ref, rows):
     bins = {}
     for k in range(KN):
         re, im = v_ref[k, rows, pl.ds(0, 128)], v_ref[k, rows, pl.ds(128, 128)]
-        tr, ti = tr_ref[pl.ds(k, 1), :], ti_ref[pl.ds(k, 1), :]
+        tr, ti = tw_ref[0, pl.ds(k, 1), :], tw_ref[1, pl.ds(k, 1), :]
         if k in (0, 64):
             bins[k] = (re * tr - im * ti, None)
         else:
@@ -240,35 +240,68 @@
 
 
 def fused_kernel(
-    up_hbm, sig_hbm, filt_hbm, hi_ref, lo_ref, tr_ref, ti_ref,
+    up_hbm, sig_hbm, filt_hbm, tab_hbm, tw_hbm,
     ig_out, fg_out,
+    tab_ref, tw_ref,
     up_x, sig_x, filt_x, up_st, sig_st, filt_st, up_in, sig_in, filt_in,
-    y_ref, u_ref, v_ref, ig_st, fg_st, ig_in, fg_in, total, fg_parts,
+    y_ref, u_ref, v_ref, ig_st, fg_st, ig_in, fg_in, fg_mid, fg_last, total, fg_parts,
     load_sem, send_sem, recv_sem,
 ):
     dp = lax.axis_index("dp")
     me = lax.axis_index("ctx")
     core, high = dp % 2, dp // 2
+    plane, place = me // 16, me % 16
     mesh_id = pl.DeviceIdType.MESH
+
+    def owner(cube, c):
+        odd = cube % 2
+        z = c // 16
+        return 16 * (odd * z + (1 - odd) * (3 - z)) + c % 16
+
+    mine = owner(high, me)
+    late = mine // 32
+    flip, mirror = high + 1 - 2 * (high % 2), 3 - high
+    first_cube = (1 - late) * flip + late * mirror
+    second_cube = (1 - late) * mirror + late * flip
+    far_cube = 3 - flip
+    reflected = (3 - plane) * 16 + place
+
     loads = [
         pltpu.make_async_copy(src, dst, load_sem.at[i])
-        for i, (src, dst) in enumerate(((up_hbm, up_x), (sig_hbm, sig_x), (filt_hbm, filt_x)))
+        for i, (src, dst) in enumerate(
+            (
+                (up_hbm, up_x), (filt_hbm, filt_x), (sig_hbm, sig_x),
+                (tab_hbm, tab_ref), (tw_hbm, tw_ref),
+            )
+        )
     ]
     for load in loads:
         load.start()
     barrier = pltpu.get_barrier_semaphore()
-    pl.semaphore_signal(barrier, inc=1, device_id=(2 * high + 1 - core, me), device_id_type=mesh_id)
-    for step in range(1, 4):
-        pl.semaphore_signal(
-            barrier, inc=1, device_id=(2 * ((high + step) % 4) + core, me), device_id_type=mesh_id
-        )
+
+    def hail(there, c):
+        pl.semaphore_signal(barrier, inc=1, device_id=(there, c), device_id_type=mesh_id)
+
+    hail(2 * high + 1 - core, me)
+    hail(2 * first_cube + core, reflected)
+    hail(2 * second_cube + core, reflected)
 
     def greet(i):
         c = partner(me, i)
         for j in range(2):
-            pl.semaphore_signal(barrier, inc=1, device_id=(2 * high + j, c), device_id_type=mesh_id)
+            hail(2 * high + j, c)
 
     loop(1, 64, greet)
+
+    def greet_outside(i):
+        step = i // 16
+        lower = 1 - plane // 2
+        z = lower * (-1 - step) + (1 - lower) * (4 + step)
+        there = (high + z // 4 + 4) % 4
+        hail(2 * there + core, (z % 4) * 16 + (place + i) % 16)
+
+    outer = 1 - (plane % 3 + 1) // 2
+    loop(0, 16 * (1 + outer), greet_outside)
 
     def turn_signal(x_ref, st_ref):
         def turn(i):
@@ -277,10 +310,11 @@
 
         loop(0, 8, turn)
 
-    def spread(src_ref, dst_ref, slot, which):
-        pltpu.make_async_copy(src_ref.at[me, core], dst_ref.at[slot], recv_sem.at[which]).start()
+    def spread(src_ref, piece, dst_ref, slot, which):
+        here = piece(me)
+        pltpu.make_async_copy(src_ref.at[here, core], dst_ref.at[slot], recv_sem.at[which]).start()
         copy_to(
-            src_ref.at[me, 1 - core], dst_ref.at[slot], send_sem.at[which], recv_sem.at[which],
+            src_ref.at[here, 1 - core], dst_ref.at[slot], send_sem.at[which], recv_sem.at[which],
             2 * high + 1 - core, me,
         ).start()
 
@@ -288,41 +322,61 @@
             c = partner(me, i)
             for j in range(2):
                 copy_to(
-                    src_ref.at[c, j], dst_ref.at[slot], send_sem.at[which], recv_sem.at[which],
-                    2 * high + j, c,
+                    src_ref.at[piece(c), j], dst_ref.at[slot], send_sem.at[which],
+                    recv_sem.at[which], 2 * high + j, c,
                 ).start()
 
         loop(1, 64, send)
 
-    def spread_same(src_ref, dst_ref, which):
-        pltpu.make_async_copy(src_ref.at[me], dst_ref.at[me], recv_sem.at[which]).start()
+    def spread_filter():
+        pltpu.make_async_copy(filt_st.at[mine], filt_in.at[me], recv_sem.at[2]).start()
+
+        def send(i):
+            there = (place + i // 4) % 16
+            even = 1 - (there // 4 + there % 4) % 2
+            ahead = i % 4
+            step = ahead - 4 * (ahead // 3) - 4 * (1 - even) * (1 - ahead % 2) * (ahead // 2)
+            z = (4 * high + plane + step + 16) % 16
+            cube = z // 4
+            c = (z % 4) * 16 + there
+            copy_to(
+                filt_st.at[owner(cube, c)], filt_in.at[me], send_sem.at[2], recv_sem.at[2],
+                2 * cube + core, c,
+            ).start()
+
+        loop(1, 64, send)
+
+    def spread_total():
+        pltpu.make_async_copy(total.at[me], fg_parts.at[mine], recv_sem.at[5]).start()
 
         def send(i):
             c = partner(me, i)
             copy_to(
-                src_ref.at[c], dst_ref.at[me], send_sem.at[which], recv_sem.at[which], dp, c
+                total.at[c], fg_parts.at[mine], send_sem.at[5], recv_sem.at[5], dp, c
             ).start()
 
         loop(1, 64, send)
 
     loads[0].wait()
     turn_signal(up_x, up_st)
-    pl.semaphore_wait(barrier, 130)
-    mine = (me, pl.ds(pl.multiple_of(32 * core, 32), 32))
-    spread(up_st, up_in, mine, 0)
+    pl.semaphore_wait(barrier, 129 + 16 * (1 + outer))
+    rows = pl.ds(pl.multiple_of(32 * core, 32), 32)
+    spread(up_st, lambda c: owner(high, c), up_in, (me, rows), 0)
     loads[1].wait()
+    loop(0, 4, lambda g: to_pieces(filt_x, filt_st, g, core, lambda owners: filt_st.at[owners]))
+    spread_filter()
+    loads[2].wait()
     turn_signal(sig_x, sig_st)
-    spread(sig_st, sig_in, mine, 1)
-    loads[2].wait()
-    loop(0, 4, lambda g: to_pieces(filt_x, filt_st, g, core, lambda owners: filt_st.at[owners]))
-    spread_same(filt_st, filt_in, 2)
+    spread(sig_st, lambda c: owner(high, c), sig_in, (me, rows), 1)
+    loads[3].wait()
+    loads[4].wait()
 
     wait_bytes(up_in, recv_sem.at[0])
-    loop(0, 4, lambda g: spectra_of(up_in, y_ref, 0, tr_ref, ti_ref, g))
+    loop(0, 4, lambda g: spectra_of(up_in, y_ref, 0, tw_ref, g))
 
     def up_spectra(step):
         k0 = step * KC
-        spec = forward_dot(y_ref, k0, 0, 64, hi_ref, lo_ref)
+        spec = forward_dot(y_ref, k0, 0, 64, tab_ref)
         for i in range(KC):
             k = k0 + i
             scale = jnp.where((k == 0) | (k == 64), 1.0 / N, 2.0 / N).astype(jnp.float32)
@@ -330,70 +384,84 @@
 
     loop(0, KN // KC, up_spectra)
 
+    wait_bytes(filt_in, recv_sem.at[2])
+    loop(0, 2, lambda g: spectra_of(filt_in, y_ref, 128, tw_ref, g))
+
+    def input_products(step):
+        k0 = step * KC
+        spec = forward_dot(y_ref, k0, 128, 32, tab_ref)
+        prods = []
+        for i in range(KC):
+            both = jnp.concatenate([spec[i], spec[i]], axis=0)
+            re, im = conj_product(both, u_ref[k0 + i])
+            prods.append(jnp.concatenate([re, im], axis=1).astype(jnp.bfloat16))
+        v_ref[pl.ds(k0, KC), pl.ds(0, 64), :] = inverse_dot(prods, tab_ref)
+
+    loop(0, KN // KC, input_products)
+
+    def input_values(group):
+        rows = pl.ds(pl.multiple_of(group * 16, 16), 16)
+        out = values_of(v_ref, tw_ref, rows)
+        kept = pl.ds(pl.multiple_of((group % 2) * 16, 16), 16)
+        for a in range(64):
+            ig_st[a, group // 2, kept, :] = out[a].astype(jnp.bfloat16)
+
+    loop(0, 4, input_values)
+    spread(ig_st, lambda c: c, ig_in, (mine, core), 4)
+
     wait_bytes(sig_in, recv_sem.at[1])
-    loop(0, 4, lambda g: spectra_of(sig_in, y_ref, 64, tr_ref, ti_ref, g))
+    loop(0, 4, lambda g: spectra_of(sig_in, y_ref, 64, tw_ref, g))
 
     def filter_products(step):
         k0 = step * KC
-        spec = forward_dot(y_ref, k0, 64, 64, hi_ref, lo_ref)
+        spec = forward_dot(y_ref, k0, 64, 64, tab_ref)
         prods = []
         for i in range(KC):
             re, im = conj_product(spec[i], u_ref[k0 + i])
             re, im = re[0:32] + re[32:64], im[0:32] + im[32:64]
             prods.append(jnp.concatenate([re, im], axis=1).astype(jnp.bfloat16))
-        v_ref[pl.ds(k0, KC), pl.ds(64, 32), :] = inverse_dot(prods, hi_ref, lo_ref)
+        v_ref[pl.ds(k0, KC), pl.ds(64, 32), :] = inverse_dot(prods, tab_ref)
 
     loop(0, KN // KC, filter_products)
 
     def filter_values(group):
         rows = pl.ds(pl.multiple_of(64 + group * 16, 16), 16)
-        out = values_of(v_ref, tr_ref, ti_ref, rows)
+        out = values_of(v_ref, tw_ref, rows)
         for a in range(0, 64, 2):
             for h in range(2):
                 pair = jnp.concatenate([out[a][8 * h:8 * h + 8], out[a + 1][8 * h:8 * h + 8]], axis=0)
                 fg_st[2 * group + h, a // 2, :, :] = pair.astype(jnp.bfloat16)
 
     loop(0, 2, filter_values)
-    for step in range(1, 4):
-        q = (high + step) % 4
-        copy_to(fg_st.at[q], fg_in.at[high], send_sem.at[3], recv_sem.at[3], 2 * q + core, me).start()
-
-    wait_bytes(filt_in, recv_sem.at[2])
-    loop(0, 2, lambda g: spectra_of(filt_in, y_ref, 128, tr_ref, ti_ref, g))
-
-    def input_products(step):
-        k0 = step * KC
-        spec = forward_dot(y_ref, k0, 128, 32, hi_ref, lo_ref)
-        prods = []
-        for i in range(KC):
-            both = jnp.concatenate([spec[i], spec[i]], axis=0)
-            re, im = conj_product(both, u_ref[k0 + i])
-            prods.append(jnp.concatenate([re, im], axis=1).astype(jnp.bfloat16))
-        v_ref[pl.ds(k0, KC), pl.ds(0, 64), :] = inverse_dot(prods, hi_ref, lo_ref)
-
-    loop(0, KN // KC, input_products)
-
-    def input_values(group):
-        rows = pl.ds(pl.multiple_of(group * 16, 16), 16)
-        out = values_of(v_ref, tr_ref, ti_ref, rows)
-        kept = pl.ds(pl.multiple_of((group % 2) * 16, 16), 16)
-        for a in range(64):
-            ig_st[a, group // 2, kept, :] = out[a].astype(jnp.bfloat16)
-
-    loop(0, 4, input_values)
-    spread(ig_st, ig_in, (me, core), 4)
-
-    wait_bytes(fg_in.at[pl.ds(0, 3)], recv_sem.at[3])
-
-    def add(p):
-        terms = fg_st[high, p].astype(jnp.float32)
-        for step in range(1, 4):
-            terms = terms + fg_in[(high + step) % 4, p].astype(jnp.float32)
+    copy_to(
+        fg_st.at[first_cube], fg_in.at[0], send_sem.at[3], recv_sem.at[3],
+        2 * first_cube + core, reflected,
+    ).start()
+    copy_to(
+        fg_st.at[far_cube], fg_in.at[1], send_sem.at[3], recv_sem.at[3],
+        2 * first_cube + core, reflected,
+    ).start()
+
+    wait_bytes(fg_in, recv_sem.at[3])
+
+    def add_half(p):
+        terms = fg_st[second_cube, p].astype(jnp.float32) + fg_in[1, p].astype(jnp.float32)
+        fg_mid[p] = terms.astype(jnp.bfloat16)
+
+    loop(0, 32, add_half)
+    copy_to(
+        fg_mid, fg_last, send_sem.at[6], recv_sem.at[6], 2 * second_cube + core, reflected
+    ).start()
+    wait_bytes(fg_last, recv_sem.at[6])
+
+    def add_last(p):
+        terms = fg_st[high, p].astype(jnp.float32) + fg_in[0, p].astype(jnp.float32)
+        terms = terms + fg_last[p].astype(jnp.float32)
         total[2 * p] = terms[0:8]
         total[2 * p + 1] = terms[8:16]
 
-    loop(0, 32, add)
-    spread_same(total, fg_parts, 5)
+    loop(0, 32, add_last)
+    spread_total()
     wait_bytes(ig_in, recv_sem.at[4])
 
     def turn_back(i):
@@ -414,7 +482,8 @@
         wait_bytes(ig_in.at[pl.ds(0, 63)], send_sem.at[which])
         wait_bytes(ig_in.at[0, 0], send_sem.at[which])
     wait_bytes(filt_in.at[pl.ds(0, 63)], send_sem.at[2])
-    wait_bytes(fg_in.at[pl.ds(0, 3)], send_sem.at[3])
+    wait_bytes(fg_in, send_sem.at[3])
+    wait_bytes(fg_mid, send_sem.at[6])
     wait_bytes(fg_parts.at[pl.ds(0, 63)], send_sem.at[5])
 
 
@@ -429,9 +498,11 @@
             jax.ShapeDtypeStruct((128, 4096), bf16),
             jax.ShapeDtypeStruct((128, 512), f32),
         ),
-        in_specs=[hbm] * 3 + [vmem] * 4,
+        in_specs=[hbm] * 5,
         out_specs=(vmem, vmem),
         scratch_shapes=[
+            pltpu.VMEM((2, 256, 256), bf16),
+            pltpu.VMEM((2, 72, 128), f32),
             pltpu.VMEM((128, 4096), bf16),
             pltpu.VMEM((128, 4096), bf16),
             pltpu.VMEM((128, 4096), bf16),
@@ -447,15 +518,17 @@
             pltpu.VMEM((64, 2, 32, 128), bf16),
             pltpu.VMEM((4, 32, 16, 128), bf16),
             pltpu.VMEM((64, 2, 32, 128), bf16),
-            pltpu.VMEM((4, 32, 16, 128), bf16),
+            pltpu.VMEM((2, 32, 16, 128), bf16),
+            pltpu.VMEM((32, 16, 128), bf16),
+            pltpu.VMEM((32, 16, 128), bf16),
             pltpu.VMEM((64, 8, 128), f32),
             pltpu.VMEM((64, 8, 128), f32),
-            pltpu.SemaphoreType.DMA((3,)),
-            pltpu.SemaphoreType.DMA((6,)),
-            pltpu.SemaphoreType.DMA((6,)),
+            pltpu.SemaphoreType.DMA((5,)),
+            pltpu.SemaphoreType.DMA((7,)),
+            pltpu.SemaphoreType.DMA((7,)),
         ],
         compiler_params=pltpu.CompilerParams(
-            collective_id=0, has_side_effects=True, vmem_limit_bytes=50 * 1024 * 1024
+            collective_id=0, has_side_effects=True, vmem_limit_bytes=60 * 1024 * 1024
         ),
     )(grad_out[0], inputs[0], filt, *tables)
     return input_grad[None], filter_grad

time: 145 us -> 132 us (0.910)
  Pallas kernels: 137 us -> 128 us
  local copies, waits for them, and re-layouts: 7.46 us -> 3.04 us
    pallas_call x1, Pallas kernels: 137 us -> 128 us  [shards(): pl.pallas_call(fused_kernel, out_shape=(jax.ShapeDtypeStruct((128, 4096),...]
    unnamed x14 -> x4, local copies, waits for them, and re-layouts: 7.46 us -> 3.04 us
where the time goes in v2:
time: 132 us; the launch traced here: 131 us
  Pallas kernels  128 us (97%)
  local copies, waits for them, and re-layouts  3.04 us (2%)
    pallas_call x1, Pallas kernels, shards(): pl.pallas_call(fused_kernel, out_shape=(jax.ShapeDtypeStruct((128, 4096),...  128 us
    unnamed x4, local copies, waits for them, and re-layouts  3.04 us

profile of v2, /device:TPU:1, one launch (start us, length us, event | category | flops | bytes accessed | tf_op | source)
XLA Modules:
  0.0 131.3 jit_solution(11203136191796466492)
XLA Ops:
  0.6 127.6 %shard_map.68 = (bf16[128,4096]{1,0:T(8,128)(2,1)}, f32[128,512]{1,0:T(8,128)}) custom-call(bf16[128,4096]{1,0:T(8,128)(2,1)} %bitcast.3, bf16[128,4096]{1,0:T(8,128)(2,1)} %bitcast.4, bf16[128,4096]{1,0:T(8,128)(2,1)} %filt_hbm.1, bf16[2,256,256]{2,1,0:T(8,128)(2,1)} %constant.4.clone.tab_hbm, f32[2,72,128]{2,1,0:T(8,128)} %constant.5.clone.tw_hbm), custom_call_target="tpu_custom_call" | custom-call | tf_op jit(solution)/shard_map/pallas_call | solution.py:495
  128.2 0.0 copy-start
  128.2 2.3 %copy.9 = bf16[1,128,4096]{2,1,0:T(8,128)(2,1)} copy(bf16[1,128,4096]{2,1,0:T(8,128)(2,1)} %bitcast.5) | data formatting | bytes 2097152
  130.5 0.0 copy-done
  130.6 0.7 copy.10
Async XLA Ops:
  128.2 2.3 %copy-start = (f32[128,512]{1,0:T(8,128)S(1)}, f32[128,512]{1,0:T(8,128)}, u32[]{:S(2)}) copy-start(f32[128,512]{1,0:T(8,128)} %get-tuple-element.9) | copy-start | bytes 786436

commit v3 on v2

--- a/solution.py
+++ b/solution.py
@@ -10,6 +10,8 @@
 N = 16384
 KN = 65
 KC = 5
+BACK_A, BACK_B = 24, 44
+QUARTERS = (0, 2, 1, 3)
 
 
 def cmul_const(v, c, s):
@@ -155,9 +157,9 @@
     return np.stack([high, low]), np.stack([np.cos(turn), np.sin(turn)]).astype(np.float32)
 
 
-def spectra_of(src_ref, y_ref, first, tw_ref, group):
+def spectra_of(src_ref, y_ref, tw_ref, group, place):
     rows = pl.ds(pl.multiple_of(group * 16, 16), 16)
-    kept = pl.ds(pl.multiple_of(first + group * 16, 16), 16)
+    kept = pl.ds(pl.multiple_of(place * 16, 16), 16)
     bins = padded_bins([src_ref[a, rows, :].astype(jnp.float32) for a in range(64)])
     for k in range(KN):
         re, im = bins[k]
@@ -224,7 +226,7 @@
 
 def to_pieces(x_ref, st_ref, g, j, index):
     parts = []
-    for q in range(4):
+    for q in QUARTERS:
         cols = pl.ds(pl.multiple_of(512 * (2 * q + j) + 128 * g, 128), 128)
         parts.append(x_ref[:, cols].astype(jnp.float32).T.reshape(16, 8, 128))
     owners = pl.ds(pl.multiple_of(16 * g, 16), 16)
@@ -311,12 +313,15 @@
         loop(0, 8, turn)
 
     def spread(src_ref, piece, dst_ref, slot, which):
-        here = piece(me)
-        pltpu.make_async_copy(src_ref.at[here, core], dst_ref.at[slot], recv_sem.at[which]).start()
-        copy_to(
-            src_ref.at[here, 1 - core], dst_ref.at[slot], send_sem.at[which], recv_sem.at[which],
-            2 * high + 1 - core, me,
-        ).start()
+        def begin():
+            here = piece(me)
+            pltpu.make_async_copy(
+                src_ref.at[here, core], dst_ref.at[slot], recv_sem.at[which]
+            ).start()
+            copy_to(
+                src_ref.at[here, 1 - core], dst_ref.at[slot], send_sem.at[which],
+                recv_sem.at[which], 2 * high + 1 - core, me,
+            ).start()
 
         def send(i):
             c = partner(me, i)
@@ -324,6 +329,29 @@
                 copy_to(
                     src_ref.at[piece(c), j], dst_ref.at[slot], send_sem.at[which],
                     recv_sem.at[which], 2 * high + j, c,
+                ).start()
+
+        return begin, send
+
+    def spread_all(*args):
+        begin, send = spread(*args)
+        begin()
+        loop(1, 64, send)
+
+    def send_signal_half(half):
+        part = pl.ds(16 * half, 16)
+        slot = (me, pl.ds(pl.multiple_of(32 * core + 16 * half, 16), 16))
+        sems = send_sem.at[7 + half], recv_sem.at[7 + half]
+        pltpu.make_async_copy(sig_st.at[mine, core, part], sig_in.at[slot], sems[1]).start()
+        copy_to(
+            sig_st.at[mine, 1 - core, part], sig_in.at[slot], *sems, 2 * high + 1 - core, me
+        ).start()
+
+        def send(i):
+            c = partner(me, i)
+            for j in range(2):
+                copy_to(
+                    sig_st.at[owner(high, c), j, part], sig_in.at[slot], *sems, 2 * high + j, c
                 ).start()
 
         loop(1, 64, send)
@@ -361,18 +389,19 @@
     turn_signal(up_x, up_st)
     pl.semaphore_wait(barrier, 129 + 16 * (1 + outer))
     rows = pl.ds(pl.multiple_of(32 * core, 32), 32)
-    spread(up_st, lambda c: owner(high, c), up_in, (me, rows), 0)
+    spread_all(up_st, lambda c: owner(high, c), up_in, (me, rows), 0)
     loads[1].wait()
     loop(0, 4, lambda g: to_pieces(filt_x, filt_st, g, core, lambda owners: filt_st.at[owners]))
     spread_filter()
     loads[2].wait()
     turn_signal(sig_x, sig_st)
-    spread(sig_st, lambda c: owner(high, c), sig_in, (me, rows), 1)
+    for half in range(2):
+        send_signal_half(half)
     loads[3].wait()
     loads[4].wait()
 
     wait_bytes(up_in, recv_sem.at[0])
-    loop(0, 4, lambda g: spectra_of(up_in, y_ref, 0, tw_ref, g))
+    loop(0, 4, lambda g: spectra_of(up_in, y_ref, tw_ref, g, g))
 
     def up_spectra(step):
         k0 = step * KC
@@ -385,7 +414,7 @@
     loop(0, KN // KC, up_spectra)
 
     wait_bytes(filt_in, recv_sem.at[2])
-    loop(0, 2, lambda g: spectra_of(filt_in, y_ref, 128, tw_ref, g))
+    loop(0, 2, lambda g: spectra_of(filt_in, y_ref, tw_ref, g, 8 + g))
 
     def input_products(step):
         k0 = step * KC
@@ -407,42 +436,45 @@
             ig_st[a, group // 2, kept, :] = out[a].astype(jnp.bfloat16)
 
     loop(0, 4, input_values)
-    spread(ig_st, lambda c: c, ig_in, (mine, core), 4)
-
-    wait_bytes(sig_in, recv_sem.at[1])
-    loop(0, 4, lambda g: spectra_of(sig_in, y_ref, 64, tw_ref, g))
-
-    def filter_products(step):
-        k0 = step * KC
-        spec = forward_dot(y_ref, k0, 64, 64, tab_ref)
-        prods = []
-        for i in range(KC):
-            re, im = conj_product(spec[i], u_ref[k0 + i])
-            re, im = re[0:32] + re[32:64], im[0:32] + im[32:64]
-            prods.append(jnp.concatenate([re, im], axis=1).astype(jnp.bfloat16))
-        v_ref[pl.ds(k0, KC), pl.ds(64, 32), :] = inverse_dot(prods, tab_ref)
-
-    loop(0, KN // KC, filter_products)
-
-    def filter_values(group):
-        rows = pl.ds(pl.multiple_of(64 + group * 16, 16), 16)
+    begin_back, send_back = spread(ig_st, lambda c: c, ig_in, (mine, core), 4)
+    begin_back()
+    loop(1, BACK_A, send_back)
+
+    def filter_half(half):
+        wait_bytes(sig_in.at[:, pl.ds(0, 32)], recv_sem.at[7 + half])
+        loop(0, 2, lambda g: spectra_of(sig_in, y_ref, tw_ref, 2 * g + half, 4 + 2 * half + g))
+        first_row = pl.multiple_of(64 + 32 * half, 32)
+        above = pl.ds(pl.multiple_of(16 * half, 16), 16)
+        below = pl.ds(pl.multiple_of(32 + 16 * half, 16), 16)
+        rows = pl.ds(pl.multiple_of(64 + 16 * half, 16), 16)
+
+        def filter_products(step):
+            k0 = step * KC
+            spec = forward_dot(y_ref, k0, first_row, 32, tab_ref)
+            prods = []
+            for i in range(KC):
+                u = jnp.concatenate([u_ref[k0 + i, above, :], u_ref[k0 + i, below, :]], axis=0)
+                re, im = conj_product(spec[i], u)
+                re, im = re[0:16] + re[16:32], im[0:16] + im[16:32]
+                prods.append(jnp.concatenate([re, im], axis=1).astype(jnp.bfloat16))
+            v_ref[pl.ds(k0, KC), rows, :] = inverse_dot(prods, tab_ref)
+
+        loop(0, KN // KC, filter_products)
         out = values_of(v_ref, tw_ref, rows)
         for a in range(0, 64, 2):
             for h in range(2):
                 pair = jnp.concatenate([out[a][8 * h:8 * h + 8], out[a + 1][8 * h:8 * h + 8]], axis=0)
-                fg_st[2 * group + h, a // 2, :, :] = pair.astype(jnp.bfloat16)
-
-    loop(0, 2, filter_values)
-    copy_to(
-        fg_st.at[first_cube], fg_in.at[0], send_sem.at[3], recv_sem.at[3],
-        2 * first_cube + core, reflected,
-    ).start()
-    copy_to(
-        fg_st.at[far_cube], fg_in.at[1], send_sem.at[3], recv_sem.at[3],
-        2 * first_cube + core, reflected,
-    ).start()
-
-    wait_bytes(fg_in, recv_sem.at[3])
+                fg_st[half + 2 * h, a // 2, :, :] = pair.astype(jnp.bfloat16)
+        far = half * (high % 2) + (1 - half) * (1 - high % 2)
+        copy_to(
+            fg_st.at[far * far_cube + (1 - far) * first_cube], fg_in.at[far],
+            send_sem.at[9 + far], recv_sem.at[9 + far], 2 * first_cube + core, reflected,
+        ).start()
+
+    loop(0, 2, filter_half)
+
+    loop(BACK_A, BACK_B, send_back)
+    wait_bytes(fg_in.at[1], recv_sem.at[10])
 
     def add_half(p):
         terms = fg_st[second_cube, p].astype(jnp.float32) + fg_in[1, p].astype(jnp.float32)
@@ -452,7 +484,9 @@
     copy_to(
         fg_mid, fg_last, send_sem.at[6], recv_sem.at[6], 2 * second_cube + core, reflected
     ).start()
+    loop(BACK_B, 64, send_back)
     wait_bytes(fg_last, recv_sem.at[6])
+    wait_bytes(fg_in.at[0], recv_sem.at[9])
 
     def add_last(p):
         terms = fg_st[high, p].astype(jnp.float32) + fg_in[0, p].astype(jnp.float32)
@@ -468,9 +502,9 @@
         g, j = i // 2, i % 2
         owners = pl.ds(pl.multiple_of(16 * g, 16), 16)
         block = ig_in[owners, j].astype(jnp.float32)
-        for q in range(4):
+        for at, q in enumerate(QUARTERS):
             cols = pl.ds(pl.multiple_of(512 * (2 * q + j) + 128 * g, 128), 128)
-            part = block[:, 8 * q : 8 * q + 8, :].reshape(128, 128)
+            part = block[:, 8 * at : 8 * at + 8, :].reshape(128, 128)
             ig_out[:, cols] = part.T.astype(jnp.bfloat16)
 
     loop(0, 8, turn_back)
@@ -478,11 +512,15 @@
     for g in range(4):
         part = fg_parts[pl.ds(16 * g, 16)].reshape(128, 128)
         fg_out[:, pl.ds(128 * g, 128)] = part.T
-    for which in (0, 1, 4):
+    for which in (7, 8):
+        wait_bytes(sig_in.at[pl.ds(0, 63), pl.ds(0, 32)], send_sem.at[which])
+        wait_bytes(sig_in.at[0, pl.ds(0, 16)], send_sem.at[which])
+    for which in (0, 4):
         wait_bytes(ig_in.at[pl.ds(0, 63)], send_sem.at[which])
         wait_bytes(ig_in.at[0, 0], send_sem.at[which])
     wait_bytes(filt_in.at[pl.ds(0, 63)], send_sem.at[2])
-    wait_bytes(fg_in, send_sem.at[3])
+    wait_bytes(fg_in.at[0], send_sem.at[9])
+    wait_bytes(fg_in.at[1], send_sem.at[10])
     wait_bytes(fg_mid, send_sem.at[6])
     wait_bytes(fg_parts.at[pl.ds(0, 63)], send_sem.at[5])
 
@@ -524,8 +562,8 @@
             pltpu.VMEM((64, 8, 128), f32),
             pltpu.VMEM((64, 8, 128), f32),
             pltpu.SemaphoreType.DMA((5,)),
-            pltpu.SemaphoreType.DMA((7,)),
-            pltpu.SemaphoreType.DMA((7,)),
+            pltpu.SemaphoreType.DMA((11,)),
+            pltpu.SemaphoreType.DMA((11,)),
         ],
         compiler_params=pltpu.CompilerParams(
             collective_id=0, has_side_effects=True, vmem_limit_bytes=60 * 1024 * 1024

time: 132 us -> 126 us (0.955)
  Pallas kernels: 128 us -> 121 us
    pallas_call x1, Pallas kernels: 128 us -> 121 us  [shards(): pl.pallas_call(fused_kernel, out_shape=(jax.ShapeDtypeStruct((128, 4096),...]
where the time goes in v3:
time: 126 us; the launch traced here: 125 us
  Pallas kernels  121 us (96%)
  local copies, waits for them, and re-layouts  3.04 us (2%)
    pallas_call x1, Pallas kernels, shards(): pl.pallas_call(fused_kernel, out_shape=(jax.ShapeDtypeStruct((128, 4096),...  121 us
    unnamed x4, local copies, waits for them, and re-layouts  3.04 us

profile of v3, /device:TPU:1, one launch (start us, length us, event | category | flops | bytes accessed | tf_op | source)
XLA Modules:
  0.0 125.1 jit_solution(2964874727847424774)
XLA Ops:
  0.6 121.4 %shard_map.68 = (bf16[128,4096]{1,0:T(8,128)(2,1)}, f32[128,512]{1,0:T(8,128)}) custom-call(bf16[128,4096]{1,0:T(8,128)(2,1)} %bitcast.3, bf16[128,4096]{1,0:T(8,128)(2,1)} %bitcast.4, bf16[128,4096]{1,0:T(8,128)(2,1)} %filt_hbm.1, bf16[2,256,256]{2,1,0:T(8,128)(2,1)} %constant.4.clone.tab_hbm, f32[2,72,128]{2,1,0:T(8,128)} %constant.5.clone.tw_hbm), custom_call_target="tpu_custom_call" | custom-call | tf_op jit(solution)/shard_map/pallas_call | solution.py:533
  122.0 0.0 copy-start
  122.0 2.3 %copy.9 = bf16[1,128,4096]{2,1,0:T(8,128)(2,1)} copy(bf16[1,128,4096]{2,1,0:T(8,128)(2,1)} %bitcast.5) | data formatting | bytes 2097152
  124.4 0.0 copy-done
  124.4 0.7 copy.10
Async XLA Ops:
  122.0 2.3 %copy-start = (f32[128,512]{1,0:T(8,128)S(1)}, f32[128,512]{1,0:T(8,128)}, u32[]{:S(2)}) copy-start(f32[128,512]{1,0:T(8,128)} %get-tuple-element.9) | copy-start | bytes 786436

commit v4 on v3

--- a/solution.py
+++ b/solution.py
@@ -9,7 +9,7 @@
 
 N = 16384
 KN = 65
-KC = 5
+KC = 13
 BACK_A, BACK_B = 24, 44
 QUARTERS = (0, 2, 1, 3)
 
@@ -477,10 +477,11 @@
     wait_bytes(fg_in.at[1], recv_sem.at[10])
 
     def add_half(p):
-        terms = fg_st[second_cube, p].astype(jnp.float32) + fg_in[1, p].astype(jnp.float32)
-        fg_mid[p] = terms.astype(jnp.bfloat16)
-
-    loop(0, 32, add_half)
+        part = pl.ds(8 * p, 8)
+        terms = fg_st[second_cube, part].astype(jnp.float32) + fg_in[1, part].astype(jnp.float32)
+        fg_mid[part] = terms.astype(jnp.bfloat16)
+
+    loop(0, 4, add_half)
     copy_to(
         fg_mid, fg_last, send_sem.at[6], recv_sem.at[6], 2 * second_cube + core, reflected
     ).start()
@@ -489,12 +490,12 @@
     wait_bytes(fg_in.at[0], recv_sem.at[9])
 
     def add_last(p):
-        terms = fg_st[high, p].astype(jnp.float32) + fg_in[0, p].astype(jnp.float32)
-        terms = terms + fg_last[p].astype(jnp.float32)
-        total[2 * p] = terms[0:8]
-        total[2 * p + 1] = terms[8:16]
-
-    loop(0, 32, add_last)
+        part = pl.ds(8 * p, 8)
+        terms = fg_st[high, part].astype(jnp.float32) + fg_in[0, part].astype(jnp.float32)
+        terms = terms + fg_last[part].astype(jnp.float32)
+        total[pl.ds(16 * p, 16)] = terms.reshape(16, 8, 128)
+
+    loop(0, 4, add_last)
     spread_total()
     wait_bytes(ig_in, recv_sem.at[4])
 

time: 126 us -> 123 us (0.976)
  Pallas kernels: 121 us -> 119 us
    pallas_call x1, Pallas kernels: 121 us -> 119 us  [shards(): pl.pallas_call(fused_kernel, out_shape=(jax.ShapeDtypeStruct((128, 4096),...]
where the time goes in v4:
time: 123 us
  Pallas kernels  119 us (97%)
  local copies, waits for them, and re-layouts  3.04 us (2%)
    pallas_call x1, Pallas kernels, shards(): pl.pallas_call(fused_kernel, out_shape=(jax.ShapeDtypeStruct((128, 4096),...  119 us
    unnamed x4, local copies, waits for them, and re-layouts  3.04 us

profile of v4, /device:TPU:1, one launch (start us, length us, event | category | flops | bytes accessed | tf_op | source)
XLA Modules:
  0.0 122.9 jit_solution(7902160344689195223)
XLA Ops:
  0.6 119.2 %shard_map.68 = (bf16[128,4096]{1,0:T(8,128)(2,1)}, f32[128,512]{1,0:T(8,128)}) custom-call(bf16[128,4096]{1,0:T(8,128)(2,1)} %bitcast.3, bf16[128,4096]{1,0:T(8,128)(2,1)} %bitcast.4, bf16[128,4096]{1,0:T(8,128)(2,1)} %filt_hbm.1, bf16[2,256,256]{2,1,0:T(8,128)(2,1)} %constant.4.clone.tab_hbm, f32[2,72,128]{2,1,0:T(8,128)} %constant.5.clone.tw_hbm), custom_call_target="tpu_custom_call" | custom-call | tf_op jit(solution)/shard_map/pallas_call | solution.py:534
  119.8 0.0 copy-start
  119.8 2.3 %copy.9 = bf16[1,128,4096]{2,1,0:T(8,128)(2,1)} copy(bf16[1,128,4096]{2,1,0:T(8,128)(2,1)} %bitcast.5) | data formatting | bytes 2097152
  122.2 0.0 copy-done
  122.2 0.7 copy.10
Async XLA Ops:
  119.8 2.3 %copy-start = (f32[128,512]{1,0:T(8,128)S(1)}, f32[128,512]{1,0:T(8,128)}, u32[]{:S(2)}) copy-start(f32[128,512]{1,0:T(8,128)} %get-tuple-element.9) | copy-start | bytes 786436

commit v5 on v4

--- a/solution.py
+++ b/solution.py
@@ -10,7 +10,7 @@
 N = 16384
 KN = 65
 KC = 13
-BACK_A, BACK_B = 24, 44
+BACK_A, BACK_B = 32, 52
 QUARTERS = (0, 2, 1, 3)
 
 
@@ -485,7 +485,6 @@
     copy_to(
         fg_mid, fg_last, send_sem.at[6], recv_sem.at[6], 2 * second_cube + core, reflected
     ).start()
-    loop(BACK_B, 64, send_back)
     wait_bytes(fg_last, recv_sem.at[6])
     wait_bytes(fg_in.at[0], recv_sem.at[9])
 
@@ -497,6 +496,7 @@
 
     loop(0, 4, add_last)
     spread_total()
+    loop(BACK_B, 64, send_back)
     wait_bytes(ig_in, recv_sem.at[4])
 
     def turn_back(i):

time: 123 us -> 122 us (level)
  no operation moved by 1% of the time
where the time goes in v5:
time: 122 us
  Pallas kernels  118 us (97%)
  local copies, waits for them, and re-layouts  3.04 us (2%)
    pallas_call x1, Pallas kernels, shards(): pl.pallas_call(fused_kernel, out_shape=(jax.ShapeDtypeStruct((128, 4096),...  118 us
    unnamed x4, local copies, waits for them, and re-layouts  3.04 us

profile of v5, /device:TPU:1, one launch (start us, length us, event | category | flops | bytes accessed | tf_op | source)
XLA Modules:
  0.0 121.8 jit_solution(14266588097306321302)
XLA Ops:
  0.6 118.1 %shard_map.68 = (bf16[128,4096]{1,0:T(8,128)(2,1)}, f32[128,512]{1,0:T(8,128)}) custom-call(bf16[128,4096]{1,0:T(8,128)(2,1)} %bitcast.3, bf16[128,4096]{1,0:T(8,128)(2,1)} %bitcast.4, bf16[128,4096]{1,0:T(8,128)(2,1)} %filt_hbm.1, bf16[2,256,256]{2,1,0:T(8,128)(2,1)} %constant.4.clone.tab_hbm, f32[2,72,128]{2,1,0:T(8,128)} %constant.5.clone.tw_hbm), custom_call_target="tpu_custom_call" | custom-call | tf_op jit(solution)/shard_map/pallas_call | solution.py:534
  118.8 0.0 copy-start
  118.8 2.3 %copy.9 = bf16[1,128,4096]{2,1,0:T(8,128)(2,1)} copy(bf16[1,128,4096]{2,1,0:T(8,128)(2,1)} %bitcast.5) | data formatting | bytes 2097152
  121.1 0.0 copy-done
  121.1 0.7 copy.10
Async XLA Ops:
  118.8 2.3 %copy-start = (f32[128,512]{1,0:T(8,128)S(1)}, f32[128,512]{1,0:T(8,128)}, u32[]{:S(2)}) copy-start(f32[128,512]{1,0:T(8,128)} %get-tuple-element.9) | copy-start | bytes 786436
